TPU v7x, 32 devices: a whole 2x2x4 slice. The times are simulated.
32 devices in a mesh: reach: 2 (over y), row: 4 (over z), col: 4 (over x, core).
Axes of the slice: x: 2, y: 2, z: 4, core: 2. Of those that a mesh axis runs over, the one named last changes fastest.
Arguments:
- operator: float32 [2048, 65536], P(('reach', 'col'), 'row'), parts along dimension 0, may hold values from -0.03125 to 0.03125
- basis: float32 [131072, 256], P(('reach', 'row')), parts along dimension 0, may hold values from -6 to 6
Outputs:
- image: float32 [2048, 256], P(('reach', 'row')), parts along dimension 0
There are 2 independent parts, one for each index of `reach`. A program takes and returns all parts, laid end to end along the dimension named above; each array names one. Nothing has to cross between parts.
All inputs are finite; a program needn't handle non-finite values.
Results may differ from a plain program's by a relative error of at most 0.000071.
Values sent between devices are 32-bit elements; how exact they have to be, the bound alone decides.
A program may use at most 64 MiB of HBM per device.

v0:
```python
import jax
import jax.numpy as jnp
from jax import lax
from jax.sharding import PartitionSpec as P


def spread(value, axis, source):
    kept = jnp.where(lax.axis_index(axis) == source, value, 0).astype(value.dtype)
    return lax.psum(kept, axis)


def shards(operator, basis):
    partial_sum = jnp.dot(
        operator, basis, preferred_element_type=jnp.float32, precision=lax.Precision.HIGHEST
    )
    tile_rows = operator.shape[0]
    n_row = lax.axis_size("row")
    n_col = lax.axis_size("col")
    group = n_row // n_col
    out_rows = tile_rows * n_col // n_row
    summed = lax.psum(partial_sum, "row")
    row_index = lax.axis_index("row")
    offset = row_index % group * out_rows
    picked = lax.dynamic_slice_in_dim(summed, offset, out_rows, 0)
    return spread(picked, "col", row_index // group)


def solution(mesh):
    in_specs = (P(("reach", "col"), "row"), P(("reach", "row"), None))
    out_specs = P(("reach", "row"), None)
    return jax.shard_map(shards, mesh=mesh, in_specs=in_specs, out_specs=out_specs, check_vma=False)
```

profile of v0, /device:TPU:0, one launch (start us, length us, event | category | flops | bytes accessed | tf_op | source)
XLA Modules:
  0.0 106.0 jit_solution(11191584294463896214)
XLA Ops:
  6.5 0.0 all-reduce.3.cloned.1.call-start
  6.5 18.6 %fusion = f32[256,256]{1,0:T(8,128)} fusion(f32[256,16384]{1,0:T(8,128)} %param.2, f32[16384,256]{1,0:T(8,128)} %param.3), kind=kOutput, calls=%fused_computation.1 | convolution fusion | flops 12884901888 | bytes 33816576 | tf_op jit(solution)/shard_map/dot_general | solution.py:13
  25.2 0.0 all-reduce.3.cloned.1.call-update
  25.2 0.0 all-reduce.5.cloned.1.call-start
  25.2 38.1 %all-reduce.3.cloned.1.call-done = f32[256,256]{1,0:T(8,128)} async-done(((f32[256,256]{1,0:T(8,128)}), f32[256,256]{1,0:T(8,128)}) %all-reduce.3.cloned.1.call-update) | async-done | bytes 262160 | tf_op jit(solution)/shard_map/psum | solution.py:21
  63.3 1.7 %broadcast_select_fusion = f32[256,256]{1,0:T(8,128)} fusion(f32[256,256]{1,0:T(8,128)} %all-reduce.3.cloned.1.call-done, pred[]{:T(512)S(6)} %eq.5), kind=kLoop, calls=%fused_computation | loop fusion | flops 65536 | bytes 524289 | tf_op jit(solution)/shard_map/jit(_where)/select_n | solution.py:8
  65.0 0.0 all-reduce.5.cloned.1.call-update
  65.0 32.5 %all-reduce.5.cloned.1.call-done = f32[256,256]{1,0:T(8,128)} async-done(((f32[256,256]{1,0:T(8,128)}), f32[256,256]{1,0:T(8,128)}) %all-reduce.5.cloned.1.call-update) | async-done | bytes 262160 | tf_op jit(solution)/shard_map/psum | solution.py:9
  97.5 1.7 %copy.5 = f32[256,256]{1,0:T(8,128)} copy(f32[256,256]{1,0:T(8,128)} %all-reduce.5.cloned.1.call-done) | data formatting | bytes 524288
Async XLA Ops:
  6.5 56.8 %all-reduce.3.cloned.1.call-start = ((), (), s32[]{:S(2)}) async-start(), calls=%async_computation | async-start | bytes 524288 | tf_op jit(solution)/shard_map/psum | solution.py:21
  25.2 72.3 %all-reduce.5.cloned.1.call-start = ((), (), s32[]{:S(2)}) async-start(), calls=%async_computation.1 | async-start | bytes 524288 | tf_op jit(solution)/shard_map/psum | solution.py:9
Sparse Core Ops, SparseCore 0:
  25.3 37.9 all-reduce.2
  65.8 31.6 all-reduce.4
where the time goes:
time: 106 us
  waiting for transfers between devices  70.6 us (67%)
  matrix products  18.6 us (18%)
  between operations  13.4 us (13%)
  other arithmetic  1.67 us (2%)
  local copies, waits for them, and re-layouts  1.67 us (2%)
    psum x1, waiting for transfers between devices, shards(): summed = lax.psum(partial_sum, 'row')  38.1 us
    psum x1, waiting for transfers between devices, spread(): return lax.psum(kept, axis)  32.5 us
    dot_general x1, matrix products, shards(): jnp.dot(operator, basis, preferred_element_type=jnp.float32, precision=la...  18.6 us
  transfers between devices with their start and end apart: 2, of which 2 were waited for; matrix products, arithmetic and copies ran while one was open for 0% of the time, Pallas kernels for 0%

commit v1 on v0

v1 whole, which is shorter than its diff:
```python
import functools

import jax
import jax.numpy as jnp
from jax import lax
from jax.experimental import pallas as pl
from jax.experimental.pallas import tpu as pltpu
from jax.sharding import PartitionSpec as P

MESH = pl.DeviceIdType.MESH
CHUNKS = (64, 64, 64, 64)
TILE = 1024


def split(values):
    high = values.astype(jnp.bfloat16)
    low = (values - high.astype(jnp.float32)).astype(jnp.bfloat16)
    return high, low


def product(a, b_high, b_low):
    rows = a.shape[0]
    high, low = split(a)
    both = jnp.dot(
        jnp.concatenate([high, low], axis=0), b_high, preferred_element_type=jnp.float32
    )
    cross = jnp.dot(high, b_low, preferred_element_type=jnp.float32)
    return both[:rows] + (both[rows:] + cross)


def kernel(
    n_row, n_col, chunks, tile,
    a_hbm, b_hbm, out_ref,
    a_ref, b_ref, b_high, b_low, part, recv,
    a_sem, b_sem, send1, recv1, send2, recv2,
):
    tile_rows, depth = a_hbm.shape
    tiles = depth // tile
    group = n_row // n_col
    out_rows = out_ref.shape[0]
    row, col = lax.axis_index("row"), lax.axis_index("col")
    home = lax.div(row, group) == col
    spans = []
    begin = 0
    for rows in chunks:
        spans.append((begin, rows))
        begin += rows
    compute = spans if group == 1 else [(0, tile_rows)]

    def load_a(index, t):
        start, rows = compute[index]
        here = (pl.ds(start, rows), pl.ds(pl.multiple_of(t * tile, tile), tile))
        return pltpu.make_async_copy(a_hbm.at[here], a_ref.at[here], a_sem.at[index, t])

    def load_b(t):
        here = pl.ds(pl.multiple_of(t * tile, tile), tile)
        return pltpu.make_async_copy(b_hbm.at[here], b_ref.at[here], b_sem.at[t])

    def first_loads(t, _):
        load_b(t).start()
        load_a(0, t).start()
        return 0

    lax.fori_loop(0, tiles, first_loads, 0)

    for index in range(1, len(compute)):
        def later_loads(t, _, index=index):
            load_a(index, t).start()
            return 0

        lax.fori_loop(0, tiles, later_loads, 0)

    barrier = pltpu.get_barrier_semaphore()
    for other in range(n_row):
        @pl.when(jnp.logical_not(home & (row == other)))
        def _(other=other):
            pl.semaphore_signal(
                barrier, inc=1, device_id={"row": other, "col": lax.div(row, group)},
                device_id_type=MESH,
            )
    for step in range(1, n_col):
        pl.semaphore_signal(
            barrier, inc=1, device_id={"row": row, "col": lax.rem(col + step, n_col)},
            device_id_type=MESH,
        )

    def scatter_copy(index, g, k):
        start, rows = spans[index]
        piece = rows // n_col
        return pltpu.make_async_remote_copy(
            src_ref=part.at[pl.ds(g * out_rows + start + k * piece, piece)],
            dst_ref=recv.at[row, pl.ds(start // n_col, piece)],
            send_sem=send1.at[index, g * n_col + k],
            recv_sem=recv1.at[index, row],
            device_id={"row": col * group + g, "col": k},
            device_id_type=MESH,
        )

    def scatter(index, wait):
        start, rows = spans[index]
        piece = rows // n_col
        for g in range(group):
            for k in range(n_col):
                mine = (col * group + g == row) & (col == k)

                @pl.when(jnp.logical_not(mine))
                def _(g=g, k=k):
                    copy = scatter_copy(index, g, k)
                    if wait:
                        copy.wait_send()
                    else:
                        copy.start()

                if not wait:
                    @pl.when(mine)
                    def _(g=g, k=k):
                        recv[row, pl.ds(start // n_col, piece)] = part[
                            pl.ds(g * out_rows + start + k * piece, piece)
                        ]

    def gather_copy(index, step):
        start, rows = spans[index]
        piece = rows // n_col
        here = out_ref.at[pl.ds(pl.multiple_of(start + col * piece, 8), piece)]
        return pltpu.make_async_remote_copy(
            src_ref=here,
            dst_ref=here,
            send_sem=send2.at[index, step],
            recv_sem=recv2.at[index, step],
            device_id={"row": row, "col": lax.rem(col + step, n_col)},
            device_id_type=MESH,
        )

    def reduce(index):
        start, rows = spans[index]
        piece = rows // n_col
        slot = pl.ds(start // n_col, piece)
        total = None
        for other in range(n_row):
            @pl.when(jnp.logical_not(home & (row == other)))
            def _(other=other):
                pltpu.make_async_remote_copy(
                    src_ref=part.at[pl.ds(start, piece)],
                    dst_ref=recv.at[other, slot],
                    send_sem=send1.at[index, 0],
                    recv_sem=recv1.at[index, other],
                    device_id={"row": other, "col": lax.div(row, group)},
                    device_id_type=MESH,
                ).wait_recv()

        for other in range(n_row):
            term = recv[other, slot]
            total = term if total is None else total + term
        out_ref[pl.ds(pl.multiple_of(start + col * piece, 8), piece)] = total
        for step in range(1, n_col):
            gather_copy(index, step).start()

    for index, (start, rows) in enumerate(compute):
        here = pl.ds(start, rows)

        def multiply(t, _, index=index, here=here):
            deep = pl.ds(pl.multiple_of(t * tile, tile), tile)
            load_a(index, t).wait()
            if index == 0:
                load_b(t).wait()
                high, low = split(b_ref[deep])
                if len(compute) > 1:
                    b_high[deep] = high
                    b_low[deep] = low
            else:
                high, low = b_high[deep], b_low[deep]
            part[here] += product(a_ref[here, deep], high, low)
            return 0

        part[here] = jnp.zeros_like(part[here])
        lax.fori_loop(0, tiles, multiply, 0)
        if index == 0:
            pl.semaphore_wait(barrier, n_row + n_col - 1 - home.astype(jnp.int32))
        scatter(index, False)
        if index > 0:
            reduce(index - 1)
    reduce(len(spans) - 1)
    for index, (start, rows) in enumerate(spans):
        piece = rows // n_col
        for step in range(1, n_col):
            owner = lax.rem(col + n_col - step, n_col)
            there = out_ref.at[pl.ds(pl.multiple_of(start + owner * piece, 8), piece)]
            pltpu.make_async_remote_copy(
                src_ref=there,
                dst_ref=there,
                send_sem=send2.at[index, step],
                recv_sem=recv2.at[index, step],
                device_id={"row": row, "col": owner},
                device_id_type=MESH,
            ).wait_recv()
    for index in range(len(spans)):
        scatter(index, True)
        for step in range(1, n_col):
            gather_copy(index, step).wait_send()


def shards(operator, basis):
    n_row = lax.axis_size("row")
    n_col = lax.axis_size("col")
    tile_rows, depth = operator.shape
    columns = basis.shape[1]
    group = n_row // n_col
    out_rows = tile_rows * n_col // n_row
    chunks = CHUNKS if group == 1 and sum(CHUNKS) == out_rows else (out_rows,)
    parts = len(chunks)
    tile = min(TILE, depth)
    tiles = depth // tile
    dma = pltpu.SemaphoreType.DMA
    split_shape = (depth, columns) if parts > 1 else (16, columns)
    return pl.pallas_call(
        functools.partial(kernel, n_row, n_col, chunks, tile),
        out_shape=jax.ShapeDtypeStruct((out_rows, columns), jnp.float32),
        in_specs=[pl.BlockSpec(memory_space=pl.ANY)] * 2,
        out_specs=pl.BlockSpec(memory_space=pltpu.VMEM),
        scratch_shapes=[
            pltpu.VMEM((tile_rows, depth), jnp.float32),
            pltpu.VMEM((depth, columns), jnp.float32),
            pltpu.VMEM(split_shape, jnp.bfloat16),
            pltpu.VMEM(split_shape, jnp.bfloat16),
            pltpu.VMEM((tile_rows, columns), jnp.float32),
            pltpu.VMEM((n_row, out_rows // n_col, columns), jnp.float32),
            dma((parts, tiles)),
            dma((tiles,)),
            dma((parts, n_row)),
            dma((parts, n_row)),
            dma((parts, n_col)),
            dma((parts, n_col)),
        ],
        compiler_params=pltpu.CompilerParams(
            collective_id=0, has_side_effects=True, vmem_limit_bytes=58 * 2**20
        ),
        cost_estimate=pl.CostEstimate(
            flops=6 * tile_rows * depth * columns,
            bytes_accessed=4 * (tile_rows * depth + depth * columns + out_rows * columns),
            transcendentals=0,
        ),
    )(operator, basis)


def solution(mesh):
    in_specs = (P(("reach", "col"), "row"), P(("reach", "row"), None))
    out_specs = P(("reach", "row"), None)
    return jax.shard_map(shards, mesh=mesh, in_specs=in_specs, out_specs=out_specs, check_vma=False)
```

time: 106 us -> 36.2 us (0.34)
  waiting for transfers between devices: 70.6 us -> 0 us
  Pallas kernels: 0 us -> 34.4 us
  matrix products: 18.6 us -> 0 us
  between operations: 13.4 us -> 0.01 us
  other arithmetic: 1.67 us -> 0 us
    psum x2 -> x0, waiting for transfers between devices: 70.6 us -> none  [the longest x1 38.1 us: shards(): summed = lax.psum(partial_sum, 'row')]
    pallas_call x0 -> x1, Pallas kernels: none -> 34.4 us  [shards(): pl.pallas_call(functools.partial(kernel, n_row, n_col, chunks, tile), out...]
    dot_general x1 -> x0, matrix products: 18.6 us -> none  [shards(): jnp.dot(operator, basis, preferred_element_type=jnp.float32, precision=la...]
    select_n x1 -> x0, other arithmetic: 1.67 us -> none  [spread(): jnp.where(lax.axis_index(axis) == source, value, 0).astype(value.dtype)]
  transfers between devices with their start and end apart: 2 -> 0, of which waited for: 2 -> 0; matrix products, arithmetic and copies ran while one was open for 0% -> 0% of each run, Pallas kernels for 0% -> 0%
where the time goes in v1:
time: 36.2 us; the launch traced here: 36.1 us
  Pallas kernels  34.4 us (95%)
  local copies, waits for them, and re-layouts  1.67 us (5%)
    pallas_call x1, Pallas kernels, shards(): pl.pallas_call(functools.partial(kernel, n_row, n_col, chunks, tile), out...  34.4 us
    unnamed x1, local copies, waits for them, and re-layouts  1.67 us

profile of v1, /device:TPU:0, one launch (start us, length us, event | category | flops | bytes accessed | tf_op | source)
XLA Modules:
  0.0 36.1 jit_solution(11674792550555870018)
XLA Ops:
  0.0 34.4 %shard_map.28 = f32[256,256]{1,0:T(8,128)} custom-call(f32[256,16384]{1,0:T(8,128)} %a_hbm.1, f32[16384,256]{1,0:T(8,128)} %b_hbm.1), custom_call_target="tpu_custom_call" | custom-call | flops 6442450944 | bytes 33816576 | tf_op jit(solution)/shard_map/pallas_call | solution.py:215
  34.4 1.7 %copy.4 = f32[256,256]{1,0:T(8,128)} copy(f32[256,256]{1,0:T(8,128)} %shard_map.28) | data formatting | bytes 524288

commit v2 on v1

--- a/solution.py
+++ b/solution.py
@@ -8,8 +8,9 @@
 from jax.sharding import PartitionSpec as P
 
 MESH = pl.DeviceIdType.MESH
-CHUNKS = (64, 64, 64, 64)
-TILE = 1024
+COMPUTE = 2
+SPANS = 4
+TILE = 2048
 
 
 def split(values):
@@ -29,7 +30,7 @@
 
 
 def kernel(
-    n_row, n_col, chunks, tile,
+    n_row, n_col, steps, parts, tile,
     a_hbm, b_hbm, out_ref,
     a_ref, b_ref, b_high, b_low, part, recv,
     a_sem, b_sem, send1, recv1, send2, recv2,
@@ -40,12 +41,10 @@
     out_rows = out_ref.shape[0]
     row, col = lax.axis_index("row"), lax.axis_index("col")
     home = lax.div(row, group) == col
-    spans = []
-    begin = 0
-    for rows in chunks:
-        spans.append((begin, rows))
-        begin += rows
-    compute = spans if group == 1 else [(0, tile_rows)]
+    step_rows, span_rows = tile_rows // steps, out_rows // parts
+    compute = [(index * step_rows, step_rows) for index in range(steps)]
+    spans = [(index * span_rows, span_rows) for index in range(parts)]
+    ratio = parts // steps
 
     def load_a(index, t):
         start, rows = compute[index]
@@ -164,7 +163,7 @@
             if index == 0:
                 load_b(t).wait()
                 high, low = split(b_ref[deep])
-                if len(compute) > 1:
+                if steps > 1:
                     b_high[deep] = high
                     b_low[deep] = low
             else:
@@ -173,13 +172,19 @@
             return 0
 
         part[here] = jnp.zeros_like(part[here])
-        lax.fori_loop(0, tiles, multiply, 0)
         if index == 0:
+            lax.fori_loop(0, tiles, multiply, 0)
             pl.semaphore_wait(barrier, n_row + n_col - 1 - home.astype(jnp.int32))
-        scatter(index, False)
-        if index > 0:
-            reduce(index - 1)
-    reduce(len(spans) - 1)
+        else:
+            middle = tiles * 3 // 4
+            lax.fori_loop(0, middle, multiply, 0)
+            for span in range((index - 1) * ratio, index * ratio):
+                reduce(span)
+            lax.fori_loop(middle, tiles, multiply, 0)
+        for span in range(index * ratio, (index + 1) * ratio):
+            scatter(span, False)
+    for span in range((steps - 1) * ratio, parts):
+        reduce(span)
     for index, (start, rows) in enumerate(spans):
         piece = rows // n_col
         for step in range(1, n_col):
@@ -206,14 +211,13 @@
     columns = basis.shape[1]
     group = n_row // n_col
     out_rows = tile_rows * n_col // n_row
-    chunks = CHUNKS if group == 1 and sum(CHUNKS) == out_rows else (out_rows,)
-    parts = len(chunks)
+    steps, parts = (COMPUTE, SPANS) if group == 1 else (1, 1)
     tile = min(TILE, depth)
     tiles = depth // tile
     dma = pltpu.SemaphoreType.DMA
-    split_shape = (depth, columns) if parts > 1 else (16, columns)
+    split_shape = (depth, columns) if steps > 1 else (16, columns)
     return pl.pallas_call(
-        functools.partial(kernel, n_row, n_col, chunks, tile),
+        functools.partial(kernel, n_row, n_col, steps, parts, tile),
         out_shape=jax.ShapeDtypeStruct((out_rows, columns), jnp.float32),
         in_specs=[pl.BlockSpec(memory_space=pl.ANY)] * 2,
         out_specs=pl.BlockSpec(memory_space=pltpu.VMEM),
@@ -224,7 +228,7 @@
             pltpu.VMEM(split_shape, jnp.bfloat16),
             pltpu.VMEM((tile_rows, columns), jnp.float32),
             pltpu.VMEM((n_row, out_rows // n_col, columns), jnp.float32),
-            dma((parts, tiles)),
+            dma((steps, tiles)),
             dma((tiles,)),
             dma((parts, n_row)),
             dma((parts, n_row)),

time: 36.2 us -> 33.8 us (0.934)
  Pallas kernels: 34.4 us -> 32 us
    pallas_call x1, Pallas kernels: 34.4 us -> 32 us  [shards(): pl.pallas_call(functools.partial(kernel, n_row, n_col, steps, parts, tile...]
where the time goes in v2:
time: 33.8 us; the launch traced here: 33.6 us
  Pallas kernels  32 us (95%)
  local copies, waits for them, and re-layouts  1.67 us (5%)
    pallas_call x1, Pallas kernels, shards(): pl.pallas_call(functools.partial(kernel, n_row, n_col, steps, parts, tile...  32 us
    unnamed x1, local copies, waits for them, and re-layouts  1.67 us

profile of v2, /device:TPU:0, one launch (start us, length us, event | category | flops | bytes accessed | tf_op | source)
XLA Modules:
  0.0 33.6 jit_solution(4093262264666394709)
XLA Ops:
  0.0 32.0 %shard_map.28 = f32[256,256]{1,0:T(8,128)} custom-call(f32[256,16384]{1,0:T(8,128)} %a_hbm.1, f32[16384,256]{1,0:T(8,128)} %b_hbm.1), custom_call_target="tpu_custom_call" | custom-call | flops 6442450944 | bytes 33816576 | tf_op jit(solution)/shard_map/pallas_call | solution.py:219
  32.0 1.7 %copy.4 = f32[256,256]{1,0:T(8,128)} copy(f32[256,256]{1,0:T(8,128)} %shard_map.28) | data formatting | bytes 524288

commit v3 on v2

--- a/solution.py
+++ b/solution.py
@@ -19,20 +19,17 @@
     return high, low
 
 
-def product(a, b_high, b_low):
-    rows = a.shape[0]
-    high, low = split(a)
-    both = jnp.dot(
-        jnp.concatenate([high, low], axis=0), b_high, preferred_element_type=jnp.float32
-    )
-    cross = jnp.dot(high, b_low, preferred_element_type=jnp.float32)
+def product(a_split, high, low):
+    rows = a_split.shape[0] // 2
+    both = jnp.dot(a_split[...], high, preferred_element_type=jnp.float32)
+    cross = jnp.dot(a_split[:rows], low, preferred_element_type=jnp.float32)
     return both[:rows] + (both[rows:] + cross)
 
 
 def kernel(
     n_row, n_col, steps, parts, tile,
     a_hbm, b_hbm, out_ref,
-    a_ref, b_ref, b_high, b_low, part, recv,
+    a_ref, b_ref, a_even, a_odd, high_even, high_odd, low_even, low_odd, part, recv,
     a_sem, b_sem, send1, recv1, send2, recv2,
 ):
     tile_rows, depth = a_hbm.shape
@@ -154,33 +151,59 @@
         for step in range(1, n_col):
             gather_copy(index, step).start()
 
-    for index, (start, rows) in enumerate(compute):
-        here = pl.ds(start, rows)
-
-        def multiply(t, _, index=index, here=here):
-            deep = pl.ds(pl.multiple_of(t * tile, tile), tile)
-            load_a(index, t).wait()
-            if index == 0:
-                load_b(t).wait()
-                high, low = split(b_ref[deep])
-                if steps > 1:
-                    b_high[deep] = high
-                    b_low[deep] = low
-            else:
-                high, low = b_high[deep], b_low[deep]
-            part[here] += product(a_ref[here, deep], high, low)
+    a_split = (a_even, a_odd)
+    b_high, b_low = (high_even, high_odd), (low_even, low_odd)
+
+    def prepare(index, t, parity):
+        start, rows = compute[index]
+        deep = pl.ds(pl.multiple_of(t * tile, tile), tile)
+        high, low = split(a_ref[pl.ds(start, rows), deep])
+        a_split[parity][:rows] = high
+        a_split[parity][rows:] = low
+        if index == 0:
+            kept = pl.ds(pl.multiple_of(lax.div(t, 2) * tile, tile), tile)
+            high, low = split(b_ref[deep])
+            b_high[parity][kept] = high
+            b_low[parity][kept] = low
+
+    def arrive(index, t):
+        load_a(index, t).wait()
+        if index == 0:
+            load_b(t).wait()
+
+    def multiply(index, t, parity):
+        here = pl.ds(*compute[index])
+        kept = pl.ds(pl.multiple_of(lax.div(t, 2) * tile, tile), tile)
+        part[here] += product(a_split[parity], b_high[parity][kept], b_low[parity][kept])
+
+    def pair(index, t, following):
+        arrive(index, t + 1)
+        if following is not None:
+            arrive(*following)
+        prepare(index, t + 1, 1)
+        multiply(index, t, 0)
+        if following is not None:
+            prepare(*following, 0)
+        multiply(index, t + 1, 1)
+
+    def pairs(index, begin, end):
+        def body(p, _):
+            pair(index, 2 * p, (index, 2 * p + 2))
             return 0
 
-        part[here] = jnp.zeros_like(part[here])
-        if index == 0:
-            lax.fori_loop(0, tiles, multiply, 0)
-            pl.semaphore_wait(barrier, n_row + n_col - 1 - home.astype(jnp.int32))
-        else:
-            middle = tiles * 3 // 4
-            lax.fori_loop(0, middle, multiply, 0)
+        lax.fori_loop(begin, end, body, 0)
+
+    part[...] = jnp.zeros_like(part)
+    arrive(0, 0)
+    prepare(0, 0, 0)
+    for index in range(steps):
+        pairs(index, 0, tiles // 2 - 1)
+        if index > 0:
             for span in range((index - 1) * ratio, index * ratio):
                 reduce(span)
-            lax.fori_loop(middle, tiles, multiply, 0)
+        pair(index, tiles - 2, (index + 1, 0) if index + 1 < steps else None)
+        if index == 0:
+            pl.semaphore_wait(barrier, n_row + n_col - 1 - home.astype(jnp.int32))
         for span in range(index * ratio, (index + 1) * ratio):
             scatter(span, False)
     for span in range((steps - 1) * ratio, parts):
@@ -212,10 +235,11 @@
     group = n_row // n_col
     out_rows = tile_rows * n_col // n_row
     steps, parts = (COMPUTE, SPANS) if group == 1 else (1, 1)
-    tile = min(TILE, depth)
+    tile = min(TILE, depth // 2)
     tiles = depth // tile
     dma = pltpu.SemaphoreType.DMA
-    split_shape = (depth, columns) if steps > 1 else (16, columns)
+    a_split = pltpu.VMEM((2 * tile_rows // steps, tile), jnp.bfloat16)
+    b_split = pltpu.VMEM((depth // 2, columns), jnp.bfloat16)
     return pl.pallas_call(
         functools.partial(kernel, n_row, n_col, steps, parts, tile),
         out_shape=jax.ShapeDtypeStruct((out_rows, columns), jnp.float32),
@@ -224,8 +248,12 @@
         scratch_shapes=[
             pltpu.VMEM((tile_rows, depth), jnp.float32),
             pltpu.VMEM((depth, columns), jnp.float32),
-            pltpu.VMEM(split_shape, jnp.bfloat16),
-            pltpu.VMEM(split_shape, jnp.bfloat16),
+            a_split,
+            a_split,
+            b_split,
+            b_split,
+            b_split,
+            b_split,
             pltpu.VMEM((tile_rows, columns), jnp.float32),
             pltpu.VMEM((n_row, out_rows // n_col, columns), jnp.float32),
             dma((steps, tiles)),

time: 33.8 us -> 35 us (1.036)
  Pallas kernels: 32 us -> 33.2 us
    pallas_call x1, Pallas kernels: 32 us -> 33.2 us  [shards(): pl.pallas_call(functools.partial(kernel, n_row, n_col, steps, parts, tile...]
where the time goes in v3:
time: 35 us; the launch traced here: 34.8 us
  Pallas kernels  33.2 us (95%)
  local copies, waits for them, and re-layouts  1.67 us (5%)
    pallas_call x1, Pallas kernels, shards(): pl.pallas_call(functools.partial(kernel, n_row, n_col, steps, parts, tile...  33.2 us
    unnamed x1, local copies, waits for them, and re-layouts  1.67 us

profile of v3, /device:TPU:0, one launch (start us, length us, event | category | flops | bytes accessed | tf_op | source)
XLA Modules:
  0.0 34.8 jit_solution(5402600867693024386)
XLA Ops:
  0.0 33.2 %shard_map.28 = f32[256,256]{1,0:T(8,128)} custom-call(f32[256,16384]{1,0:T(8,128)} %a_hbm.1, f32[16384,256]{1,0:T(8,128)} %b_hbm.1), custom_call_target="tpu_custom_call" | custom-call | flops 6442450944 | bytes 33816576 | tf_op jit(solution)/shard_map/pallas_call | solution.py:243
  33.2 1.7 %copy.4 = f32[256,256]{1,0:T(8,128)} copy(f32[256,256]{1,0:T(8,128)} %shard_map.28) | data formatting | bytes 524288

commit v4 on v2

v4 whole, which is shorter than its diff:
```python
import functools

import jax
import jax.numpy as jnp
from jax import lax
from jax.experimental import pallas as pl
from jax.experimental.pallas import tpu as pltpu
from jax.sharding import PartitionSpec as P

MESH = pl.DeviceIdType.MESH
COMPUTE = 2
SPANS = 4
TILE = 2048


def split(values):
    high = values.astype(jnp.bfloat16)
    low = (values - high.astype(jnp.float32)).astype(jnp.bfloat16)
    return high, low


def product(a, b_high, b_low):
    rows = a.shape[0]
    high, low = split(a)
    both = jnp.dot(
        jnp.concatenate([high, low], axis=0), b_high, preferred_element_type=jnp.float32
    )
    cross = jnp.dot(high, b_low, preferred_element_type=jnp.float32)
    return both[:rows] + (both[rows:] + cross)


def kernel(
    n_row, n_col, steps, parts, tile,
    a_hbm, b_hbm, out_ref,
    a_ref, b_ref, b_high, b_low, part, mid, recv,
    a_sem, b_sem, send1, recv1, send2, recv2, send3, recv3,
):
    tile_rows, depth = a_hbm.shape
    tiles = depth // tile
    group = n_row // n_col
    out_rows = out_ref.shape[0]
    row, col = lax.axis_index("row"), lax.axis_index("col")
    step_rows, span_rows = tile_rows // steps, out_rows // parts
    compute = [(index * step_rows, step_rows) for index in range(steps)]
    spans = [(index * span_rows, span_rows) for index in range(parts)]
    ratio = parts // steps

    def load_a(index, t):
        start, rows = compute[index]
        here = (pl.ds(start, rows), pl.ds(pl.multiple_of(t * tile, tile), tile))
        return pltpu.make_async_copy(a_hbm.at[here], a_ref.at[here], a_sem.at[index, t])

    def load_b(t):
        here = pl.ds(pl.multiple_of(t * tile, tile), tile)
        return pltpu.make_async_copy(b_hbm.at[here], b_ref.at[here], b_sem.at[t])

    def first_loads(t, _):
        load_b(t).start()
        load_a(0, t).start()
        return 0

    lax.fori_loop(0, tiles, first_loads, 0)

    for index in range(1, len(compute)):
        def later_loads(t, _, index=index):
            load_a(index, t).start()
            return 0

        lax.fori_loop(0, tiles, later_loads, 0)

    barrier = pltpu.get_barrier_semaphore()
    for step in range(1, n_col):
        pl.semaphore_signal(
            barrier, inc=1, device_id={"row": row, "col": lax.rem(col + step, n_col)},
            device_id_type=MESH,
        )
    for step in range(1, n_row):
        pl.semaphore_signal(
            barrier, inc=1, device_id={"row": lax.rem(row + step, n_row), "col": col},
            device_id_type=MESH,
        )

    def piece_of(index):
        start, rows = spans[index]
        return start, rows // n_col, pl.ds(start // n_col, rows // n_col)

    def stage1(index, step, g):
        start, piece, slot = piece_of(index)
        other = lax.rem(col + step, n_col)
        first = pl.multiple_of(g * out_rows + start + other * piece, 8)
        return pltpu.make_async_remote_copy(
            src_ref=part.at[pl.ds(first, piece)],
            dst_ref=mid.at[col * group + g, slot],
            send_sem=send1.at[index, step * group + g],
            recv_sem=recv1.at[index, step * group + g],
            device_id={"row": row, "col": other},
            device_id_type=MESH,
        )

    def arrive1(index, step, g):
        start, piece, slot = piece_of(index)
        other = lax.rem(col + n_col - step, n_col)
        pltpu.make_async_remote_copy(
            src_ref=part.at[pl.ds(start, piece)],
            dst_ref=mid.at[other * group + g, slot],
            send_sem=send1.at[index, step * group + g],
            recv_sem=recv1.at[index, step * group + g],
            device_id={"row": row, "col": other},
            device_id_type=MESH,
        ).wait_recv()

    def stage2(index, step):
        slot = piece_of(index)[2]
        other = lax.rem(row + step, n_row)
        return pltpu.make_async_remote_copy(
            src_ref=mid.at[other, slot],
            dst_ref=recv.at[step, slot],
            send_sem=send2.at[index, step],
            recv_sem=recv2.at[index, step],
            device_id={"row": other, "col": col},
            device_id_type=MESH,
        )

    def stage3(index, step):
        start, piece, _ = piece_of(index)
        here = out_ref.at[pl.ds(pl.multiple_of(start + col * piece, 8), piece)]
        return pltpu.make_async_remote_copy(
            src_ref=here,
            dst_ref=here,
            send_sem=send3.at[index, step],
            recv_sem=recv3.at[index, step],
            device_id={"row": row, "col": lax.rem(col + step, n_col)},
            device_id_type=MESH,
        )

    def arrive3(index, step):
        start, piece, _ = piece_of(index)
        other = lax.rem(col + n_col - step, n_col)
        there = out_ref.at[pl.ds(pl.multiple_of(start + other * piece, 8), piece)]
        pltpu.make_async_remote_copy(
            src_ref=there,
            dst_ref=there,
            send_sem=send3.at[index, step],
            recv_sem=recv3.at[index, step],
            device_id={"row": row, "col": other},
            device_id_type=MESH,
        ).wait_recv()

    def scatter(index):
        start, piece, slot = piece_of(index)
        for step in range(1, n_col):
            for g in range(group):
                stage1(index, step, g).start()
        for g in range(group):
            first = pl.multiple_of(g * out_rows + start + col * piece, 8)
            mid[col * group + g, slot] = part[pl.ds(first, piece)]

    def forward(index):
        for step in range(1, n_col):
            for g in range(group):
                arrive1(index, step, g)
        for step in range(1, n_row):
            stage2(index, step).start()

    def reduce(index):
        start, piece, slot = piece_of(index)
        total = mid[row, slot]
        for step in range(1, n_row):
            stage2(index, step).wait_recv()
            total = total + recv[step, slot]
        out_ref[pl.ds(pl.multiple_of(start + col * piece, 8), piece)] = total
        for step in range(1, n_col):
            stage3(index, step).start()

    for index, (start, rows) in enumerate(compute):
        here = pl.ds(start, rows)

        def multiply(t, _, index=index, here=here):
            deep = pl.ds(pl.multiple_of(t * tile, tile), tile)
            load_a(index, t).wait()
            if index == 0:
                load_b(t).wait()
                high, low = split(b_ref[deep])
                if steps > 1:
                    b_high[deep] = high
                    b_low[deep] = low
            else:
                high, low = b_high[deep], b_low[deep]
            part[here] += product(a_ref[here, deep], high, low)
            return 0

        part[here] = jnp.zeros_like(part[here])
        middle = tiles // 2 if index > 0 else 0
        lax.fori_loop(0, middle, multiply, 0)
        if index > 0:
            for span in range((index - 1) * ratio, index * ratio):
                forward(span)
        lax.fori_loop(middle, tiles, multiply, 0)
        if index == 0:
            pl.semaphore_wait(barrier, n_row + n_col - 2)
        for span in range(index * ratio, (index + 1) * ratio):
            scatter(span)
        if index > 0:
            for span in range((index - 1) * ratio, index * ratio):
                reduce(span)
    for span in range((steps - 1) * ratio, parts):
        forward(span)
    for span in range((steps - 1) * ratio, parts):
        reduce(span)
    for span in range(parts):
        for step in range(1, n_col):
            arrive3(span, step)
    for span in range(parts):
        for step in range(1, n_col):
            for g in range(group):
                stage1(span, step, g).wait_send()
            stage3(span, step).wait_send()
        for step in range(1, n_row):
            stage2(span, step).wait_send()


def shards(operator, basis):
    n_row = lax.axis_size("row")
    n_col = lax.axis_size("col")
    tile_rows, depth = operator.shape
    columns = basis.shape[1]
    group = n_row // n_col
    out_rows = tile_rows * n_col // n_row
    steps, parts = (COMPUTE, SPANS) if group == 1 else (1, 1)
    tile = min(TILE, depth)
    tiles = depth // tile
    dma = pltpu.SemaphoreType.DMA
    split_shape = (depth, columns) if steps > 1 else (16, columns)
    return pl.pallas_call(
        functools.partial(kernel, n_row, n_col, steps, parts, tile),
        out_shape=jax.ShapeDtypeStruct((out_rows, columns), jnp.float32),
        in_specs=[pl.BlockSpec(memory_space=pl.ANY)] * 2,
        out_specs=pl.BlockSpec(memory_space=pltpu.VMEM),
        scratch_shapes=[
            pltpu.VMEM((tile_rows, depth), jnp.float32),
            pltpu.VMEM((depth, columns), jnp.float32),
            pltpu.VMEM(split_shape, jnp.bfloat16),
            pltpu.VMEM(split_shape, jnp.bfloat16),
            pltpu.VMEM((tile_rows, columns), jnp.float32),
            pltpu.VMEM((n_row, out_rows // n_col, columns), jnp.float32),
            pltpu.VMEM((n_row, out_rows // n_col, columns), jnp.float32),
            dma((steps, tiles)),
            dma((tiles,)),
            dma((parts, n_row)),
            dma((parts, n_row)),
            dma((parts, n_row)),
            dma((parts, n_row)),
            dma((parts, n_col)),
            dma((parts, n_col)),
        ],
        compiler_params=pltpu.CompilerParams(
            collective_id=0, has_side_effects=True, vmem_limit_bytes=58 * 2**20
        ),
        cost_estimate=pl.CostEstimate(
            flops=6 * tile_rows * depth * columns,
            bytes_accessed=4 * (tile_rows * depth + depth * columns + out_rows * columns),
            transcendentals=0,
        ),
    )(operator, basis)


def solution(mesh):
    in_specs = (P(("reach", "col"), "row"), P(("reach", "row"), None))
    out_specs = P(("reach", "row"), None)
    return jax.shard_map(shards, mesh=mesh, in_specs=in_specs, out_specs=out_specs, check_vma=False)
```

time: 33.8 us -> 32 us (0.947)
  Pallas kernels: 32 us -> 30.2 us
    pallas_call x1, Pallas kernels: 32 us -> 30.2 us  [shards(): pl.pallas_call(functools.partial(kernel, n_row, n_col, steps, parts, tile...]
where the time goes in v4:
time: 32 us; the launch traced here: 31.8 us
  Pallas kernels  30.2 us (94%)
  local copies, waits for them, and re-layouts  1.67 us (5%)
    pallas_call x1, Pallas kernels, shards(): pl.pallas_call(functools.partial(kernel, n_row, n_col, steps, parts, tile...  30.2 us
    unnamed x1, local copies, waits for them, and re-layouts  1.67 us

profile of v4, /device:TPU:0, one launch (start us, length us, event | category | flops | bytes accessed | tf_op | source)
XLA Modules:
  0.0 31.8 jit_solution(10225471069738473850)
XLA Ops:
  0.0 30.2 %shard_map.28 = f32[256,256]{1,0:T(8,128)} custom-call(f32[256,16384]{1,0:T(8,128)} %a_hbm.1, f32[16384,256]{1,0:T(8,128)} %b_hbm.1), custom_call_target="tpu_custom_call" | custom-call | flops 6442450944 | bytes 33816576 | tf_op jit(solution)/shard_map/pallas_call | solution.py:234
  30.2 1.7 %copy.4 = f32[256,256]{1,0:T(8,128)} copy(f32[256,256]{1,0:T(8,128)} %shard_map.28) | data formatting | bytes 524288

commit v5 on v4

--- a/solution.py
+++ b/solution.py
@@ -20,13 +20,9 @@
 
 
 def product(a, b_high, b_low):
-    rows = a.shape[0]
     high, low = split(a)
-    both = jnp.dot(
-        jnp.concatenate([high, low], axis=0), b_high, preferred_element_type=jnp.float32
-    )
-    cross = jnp.dot(high, b_low, preferred_element_type=jnp.float32)
-    return both[:rows] + (both[rows:] + cross)
+    dot = functools.partial(jnp.dot, preferred_element_type=jnp.float32)
+    return dot(high, b_high) + (dot(low, b_high) + dot(high, b_low))
 
 
 def kernel(

time: 32 us -> 31.9 us (level)
  no operation moved by 1% of the time
where the time goes in v5:
time: 31.9 us; the launch traced here: 31.8 us
  Pallas kernels  30.1 us (94%)
  local copies, waits for them, and re-layouts  1.67 us (5%)
    pallas_call x1, Pallas kernels, shards(): pl.pallas_call(functools.partial(kernel, n_row, n_col, steps, parts, tile...  30.1 us
    unnamed x1, local copies, waits for them, and re-layouts  1.67 us

profile of v5, /device:TPU:0, one launch (start us, length us, event | category | flops | bytes accessed | tf_op | source)
XLA Modules:
  0.0 31.8 jit_solution(14533441943370971897)
XLA Ops:
  0.0 30.1 %shard_map.28 = f32[256,256]{1,0:T(8,128)} custom-call(f32[256,16384]{1,0:T(8,128)} %a_hbm.1, f32[16384,256]{1,0:T(8,128)} %b_hbm.1), custom_call_target="tpu_custom_call" | custom-call | flops 6442450944 | bytes 33816576 | tf_op jit(solution)/shard_map/pallas_call | solution.py:230
  30.1 1.7 %copy.4 = f32[256,256]{1,0:T(8,128)} copy(f32[256,256]{1,0:T(8,128)} %shard_map.28) | data formatting | bytes 524288

commit v6 on v4

--- a/solution.py
+++ b/solution.py
@@ -10,7 +10,7 @@
 MESH = pl.DeviceIdType.MESH
 COMPUTE = 2
 SPANS = 4
-TILE = 2048
+TILE = 1024
 
 
 def split(values):
@@ -190,7 +190,7 @@
             return 0
 
         part[here] = jnp.zeros_like(part[here])
-        middle = tiles // 2 if index > 0 else 0
+        middle = tiles * 3 // 8 if index > 0 else 0
         lax.fori_loop(0, middle, multiply, 0)
         if index > 0:
             for span in range((index - 1) * ratio, index * ratio):

time: 32 us -> 33.3 us (1.041)
  Pallas kernels: 30.2 us -> 31.5 us
    pallas_call x1, Pallas kernels: 30.2 us -> 31.5 us  [shards(): pl.pallas_call(functools.partial(kernel, n_row, n_col, steps, parts, tile...]
where the time goes in v6:
time: 33.3 us; the launch traced here: 33.2 us
  Pallas kernels  31.5 us (95%)
  local copies, waits for them, and re-layouts  1.67 us (5%)
    pallas_call x1, Pallas kernels, shards(): pl.pallas_call(functools.partial(kernel, n_row, n_col, steps, parts, tile...  31.5 us
    unnamed x1, local copies, waits for them, and re-layouts  1.67 us

profile of v6, /device:TPU:0, one launch (start us, length us, event | category | flops | bytes accessed | tf_op | source)
XLA Modules:
  0.0 33.2 jit_solution(2880888210278427921)
XLA Ops:
  0.0 31.5 %shard_map.28 = f32[256,256]{1,0:T(8,128)} custom-call(f32[256,16384]{1,0:T(8,128)} %a_hbm.1, f32[16384,256]{1,0:T(8,128)} %b_hbm.1), custom_call_target="tpu_custom_call" | custom-call | flops 6442450944 | bytes 33816576 | tf_op jit(solution)/shard_map/pallas_call | solution.py:234
  31.5 1.7 %copy.4 = f32[256,256]{1,0:T(8,128)} copy(f32[256,256]{1,0:T(8,128)} %shard_map.28) | data formatting | bytes 524288

commit v7 on v4

--- a/solution.py
+++ b/solution.py
@@ -45,9 +45,13 @@
     spans = [(index * span_rows, span_rows) for index in range(parts)]
     ratio = parts // steps
 
+    def deep_of(index):
+        return tile if index == 0 else 2 * tile
+
     def load_a(index, t):
         start, rows = compute[index]
-        here = (pl.ds(start, rows), pl.ds(pl.multiple_of(t * tile, tile), tile))
+        deep = deep_of(index)
+        here = (pl.ds(start, rows), pl.ds(pl.multiple_of(t * deep, deep), deep))
         return pltpu.make_async_copy(a_hbm.at[here], a_ref.at[here], a_sem.at[index, t])
 
     def load_b(t):
@@ -66,7 +70,7 @@
             load_a(index, t).start()
             return 0
 
-        lax.fori_loop(0, tiles, later_loads, 0)
+        lax.fori_loop(0, tiles // 2, later_loads, 0)
 
     barrier = pltpu.get_barrier_semaphore()
     for step in range(1, n_col):
@@ -176,7 +180,7 @@
         here = pl.ds(start, rows)
 
         def multiply(t, _, index=index, here=here):
-            deep = pl.ds(pl.multiple_of(t * tile, tile), tile)
+            deep = pl.ds(pl.multiple_of(t * deep_of(index), deep_of(index)), deep_of(index))
             load_a(index, t).wait()
             if index == 0:
                 load_b(t).wait()
@@ -190,12 +194,13 @@
             return 0
 
         part[here] = jnp.zeros_like(part[here])
-        middle = tiles // 2 if index > 0 else 0
+        turns = tiles if index == 0 else tiles // 2
+        middle = turns // 2 if index > 0 else 0
         lax.fori_loop(0, middle, multiply, 0)
         if index > 0:
             for span in range((index - 1) * ratio, index * ratio):
                 forward(span)
-        lax.fori_loop(middle, tiles, multiply, 0)
+        lax.fori_loop(middle, turns, multiply, 0)
         if index == 0:
             pl.semaphore_wait(barrier, n_row + n_col - 2)
         for span in range(index * ratio, (index + 1) * ratio):

time: 32 us -> 31.6 us (0.988)
  Pallas kernels: 30.2 us -> 29.8 us
    pallas_call x1, Pallas kernels: 30.2 us -> 29.8 us  [shards(): pl.pallas_call(functools.partial(kernel, n_row, n_col, steps, parts, tile...]
where the time goes in v7:
time: 31.6 us; the launch traced here: 31.5 us
  Pallas kernels  29.8 us (94%)
  local copies, waits for them, and re-layouts  1.67 us (5%)
    pallas_call x1, Pallas kernels, shards(): pl.pallas_call(functools.partial(kernel, n_row, n_col, steps, parts, tile...  29.8 us
    unnamed x1, local copies, waits for them, and re-layouts  1.67 us

profile of v7, /device:TPU:0, one launch (start us, length us, event | category | flops | bytes accessed | tf_op | source)
XLA Modules:
  0.0 31.5 jit_solution(16921844420594291843)
XLA Ops:
  0.0 29.8 %shard_map.28 = f32[256,256]{1,0:T(8,128)} custom-call(f32[256,16384]{1,0:T(8,128)} %a_hbm.1, f32[16384,256]{1,0:T(8,128)} %b_hbm.1), custom_call_target="tpu_custom_call" | custom-call | flops 6442450944 | bytes 33816576 | tf_op jit(solution)/shard_map/pallas_call | solution.py:239
  29.8 1.7 %copy.4 = f32[256,256]{1,0:T(8,128)} copy(f32[256,256]{1,0:T(8,128)} %shard_map.28) | data formatting | bytes 524288
